TPU v7x, 32 devices: a whole 2x2x4 slice. The times are simulated.
32 devices in a mesh: dp: 2 (over x), ctx: 4 (over z), tp: 4 (over y, core).
Axes of the slice: x: 2, y: 2, z: 4, core: 2. Of those that a mesh axis runs over, the one named last changes fastest.
Arguments:
- tokens: bfloat16 [2, 2048, 2048], P('dp', ('ctx', 'tp')), may hold values from -6 to 6
- attn_gain: float32 [2048], replicated, may hold values from 0.25 to 1.75
- w_query: bfloat16 [2048, 2048], P(None, 'tp'), may hold values from -0.1875 to 0.1875
- w_key: bfloat16 [2048, 512], P(None, 'tp'), may hold values from -0.1875 to 0.1875
- w_value: bfloat16 [2048, 512], P(None, 'tp'), may hold values from -0.125 to 0.125
- w_out: bfloat16 [2048, 2048], P('tp'), may hold values from -0.75 to 0.75
- ffn_gain: float32 [2048], replicated, may hold values from 0.25 to 1.75
- w_gate: bfloat16 [2048, 8192], P(None, 'tp'), may hold values from -0.125 to 0.125
- w_up: bfloat16 [2048, 8192], P(None, 'tp'), may hold values from -0.125 to 0.125
- w_down: bfloat16 [8192, 2048], P('tp'), may hold values from -0.0625 to 0.0625
- out_cotangent: bfloat16 [2, 2048, 2048], P('dp', ('ctx', 'tp')), may hold values from -6 to 6
- doc_lengths: int32 [2, 8], P('dp'), may hold values from 1 to 1408, as said below
Outputs:
- layer_out: bfloat16 [2, 2048, 2048], P('dp', ('ctx', 'tp'))
- input_grad: float32 [2, 2048, 2048], P('dp', ('ctx', 'tp'))
- grad_attn_gain: float32 [2048], replicated
- grad_w_query: float32 [2048, 2048], P(('dp', 'ctx'), 'tp')
- grad_w_key: float32 [2048, 512], P(('dp', 'ctx'), 'tp')
- grad_w_value: float32 [2048, 512], P(('dp', 'ctx'), 'tp')
- grad_w_out: float32 [2048, 2048], P('tp', ('dp', 'ctx'))
- grad_ffn_gain: float32 [2048], replicated
- grad_w_gate: float32 [2048, 8192], P(('dp', 'ctx'), 'tp')
- grad_w_up: float32 [2048, 8192], P(('dp', 'ctx'), 'tp')
- grad_w_down: float32 [8192, 2048], P('tp', ('dp', 'ctx'))
Inputs may be any that keep to these rules, and one draw needn't show every extreme that they name: `doc_lengths`: each row holds its 8 documents in this order from position 0, then padding. The first has exactly 1408 tokens, the others at least one; together they leave 1 to 255 padding positions.
All inputs are finite; a program needn't handle non-finite values.
Results may differ from a plain program's by a relative error of at most 0.024.
Values may be sent and summed in bfloat16 or wider, within the bound.
No kernel may reach another device: no remote copies, remote signals or barrier semaphores. Data moves between devices by JAX's collectives and lax.ppermute only.
A program may use at most 192 MiB of HBM per device.

v0:
```python
import math

import jax
import jax.numpy as jnp
import numpy as np
from jax import lax
from jax.sharding import PartitionSpec as P

HD = 64


EPSILON = 1e-05
NEGATIVE = -1e30
START_MAX = -1e20
ROPE_THETA = 500000.0


def rope_table(head_size):
    base_freq = np.array(
        [ROPE_THETA ** (-2.0 * index / head_size) for index in range(head_size // 2)]
    )
    wavelength = 2.0 * math.pi / base_freq
    blend = (8192.0 / wavelength - 1.0) / 3.0
    middle = (1.0 - blend) * base_freq / 32.0 + blend * base_freq
    return np.where(
        wavelength > 8192.0, base_freq / 32.0, np.where(wavelength < 2048.0, base_freq, middle)
    )


def stored_positions(first_row, row_count, ctx_rows, ctx_count):
    stored = first_row + jnp.arange(row_count, dtype=jnp.int32)
    owner = stored // ctx_rows
    within = stored % ctx_rows
    half_rows = ctx_rows // 2
    piece_num = jnp.where(within < half_rows, owner, 2 * ctx_count - 1 - owner)
    return (piece_num * half_rows + within % half_rows).astype(jnp.int32)


def doc_segments(positions, doc_row):
    ends = jnp.cumsum(doc_row)
    return jnp.sum((positions[:, None] >= ends[None, :]).astype(jnp.int32), axis=1)


def rms_norm(values_in, gain_vec):
    return (
        values_in
        * lax.rsqrt(jnp.mean(values_in * values_in, axis=-1, keepdims=True) + EPSILON)
        * gain_vec
    )


def rotate(values_in, cosine, sine_part):
    halfway = values_in.shape[-1] // 2
    first_half = values_in[..., :halfway]
    second_half = values_in[..., halfway:]
    return jnp.concatenate(
        [
            first_half * cosine - second_half * sine_part,
            second_half * cosine + first_half * sine_part,
        ],
        axis=-1,
    )


def unrotate(values_in, cosine, sine_part):
    halfway = values_in.shape[-1] // 2
    first_half = values_in[..., :halfway]
    second_half = values_in[..., halfway:]
    return jnp.concatenate(
        [
            first_half * cosine + second_half * sine_part,
            second_half * cosine - first_half * sine_part,
        ],
        axis=-1,
    )


def contract_rows(left, right):
    return lax.dot_general(
        left, right, (((0,), (0,)), ((), ())), preferred_element_type=jnp.float32
    )


def contract_cols(left, right):
    return lax.dot_general(
        left, right, (((1,), (1,)), ((), ())), preferred_element_type=jnp.float32
    )


def per_device(
    tokens,
    attn_gain,
    w_query,
    w_key,
    w_value,
    w_out,
    ffn_gain,
    w_gate,
    w_up,
    w_down,
    out_cotangent,
    doc_lengths,
):
    ctx_count = lax.axis_size("ctx")
    tp_rows = tokens.shape[1]
    ctx_rows = tp_rows * lax.axis_size("tp")
    kv_heads = w_key.shape[1] // HD
    q_heads = w_query.shape[1] // HD
    per_group = q_heads // kv_heads
    query_rows = per_group * ctx_rows
    score_scale = 1.0 / math.sqrt(HD)
    doc_row = doc_lengths[0]
    ctx_start = lax.axis_index("ctx") * ctx_rows
    query_pos = stored_positions(ctx_start, ctx_rows, ctx_rows, ctx_count)
    query_seg = doc_segments(query_pos, doc_row)
    is_valid = (query_seg < doc_row.shape[0]).astype(jnp.float32)
    row_pos = jnp.tile(query_pos, per_group)
    row_seg = jnp.tile(query_seg, per_group)
    valid_rows = jnp.tile(is_valid, per_group)
    inv_freq = jnp.asarray(rope_table(HD), jnp.float32)
    angles = query_pos.astype(jnp.float32)[:, None] * inv_freq[None, :]
    cosine = jnp.cos(angles)[:, None, :]
    sine_part = jnp.sin(angles)[:, None, :]
    inputs = tokens[0].astype(jnp.float32)
    normed_local = rms_norm(inputs, attn_gain).astype(jnp.bfloat16)
    normed = lax.all_gather(normed_local, "tp", axis=0, tiled=True)
    queries = jnp.dot(normed, w_query, preferred_element_type=jnp.float32).reshape(
        ctx_rows, q_heads, HD
    )
    keys_raw = jnp.dot(normed, w_key, preferred_element_type=jnp.float32).reshape(
        ctx_rows, kv_heads, HD
    )
    values = (
        jnp.dot(normed, w_value, preferred_element_type=jnp.float32)
        .astype(jnp.bfloat16)
        .reshape(ctx_rows, kv_heads, HD)
    )
    rot_queries = rotate(queries, cosine, sine_part).astype(jnp.bfloat16)
    rot_keys = rotate(keys_raw, cosine, sine_part).astype(jnp.bfloat16)
    query_mat = (
        rot_queries.reshape(ctx_rows, kv_heads, per_group, HD)
        .transpose(1, 2, 0, 3)
        .reshape(kv_heads, query_rows, HD)
    )

    def scores_of(key_blk, first_row):
        raw_scores = (
            jnp.einsum("hrd,khd->hrk", query_mat, key_blk, preferred_element_type=jnp.float32)
            * score_scale
        )
        key_pos = stored_positions(first_row, key_blk.shape[0], ctx_rows, ctx_count)
        key_seg = doc_segments(key_pos, doc_row)
        allowed = (row_seg[:, None] == key_seg[None, :]) & (key_pos[None, :] <= row_pos[:, None])
        return (jnp.where(allowed[None], raw_scores, NEGATIVE), allowed)

    def absorb(state_in, key_blk, value_blk, first_row):
        row_max, row_sum, weighted = state_in
        scores, allowed = scores_of(key_blk, first_row)
        new_max = jnp.maximum(row_max, jnp.max(scores, axis=2))
        rescale = jnp.exp(row_max - new_max)
        expo = jnp.where(allowed[None], jnp.exp(scores - new_max[:, :, None]), 0.0)
        row_sum = row_sum * rescale + jnp.sum(expo, axis=2)
        weighted = weighted * rescale[:, :, None] + jnp.einsum(
            "hrk,khd->hrd", expo.astype(jnp.bfloat16), value_blk, preferred_element_type=jnp.float32
        )
        return (new_max, row_sum, weighted)

    empty = (
        jnp.full((kv_heads, query_rows), START_MAX, jnp.float32),
        jnp.zeros((kv_heads, query_rows), jnp.float32),
        jnp.zeros((kv_heads, query_rows, HD), jnp.float32),
    )
    first_row = jnp.int32(0)
    key_part = lax.all_gather(rot_keys, "ctx", axis=0, tiled=True)
    value_part = lax.all_gather(values, "ctx", axis=0, tiled=True)
    step_rows = math.gcd(key_part.shape[0], ctx_rows)

    def one_step(step_num, inner):
        offset = step_num * step_rows
        key_blk = lax.dynamic_slice_in_dim(key_part, offset, step_rows, 0)
        value_blk = lax.dynamic_slice_in_dim(value_part, offset, step_rows, 0)
        return absorb(inner, key_blk, value_blk, first_row + offset)

    row_max, row_sum, weighted = lax.fori_loop(0, key_part.shape[0] // step_rows, one_step, empty)
    attended = weighted / row_sum[:, :, None]
    log_total = row_max + jnp.log(row_sum)
    merged_heads = (attended * valid_rows[None, :, None]).astype(jnp.bfloat16)
    merged = (
        merged_heads.reshape(kv_heads, per_group, ctx_rows, HD)
        .transpose(2, 0, 1, 3)
        .reshape(ctx_rows, q_heads * HD)
    )
    hidden_state = inputs + lax.psum_scatter(
        jnp.dot(merged, w_out, preferred_element_type=jnp.float32).astype(jnp.bfloat16),
        "tp",
        scatter_dimension=0,
        tiled=True,
    ).astype(jnp.float32)
    normed_ffn_local = rms_norm(hidden_state, ffn_gain).astype(jnp.bfloat16)
    normed_ffn = lax.all_gather(normed_ffn_local, "tp", axis=0, tiled=True)
    gate = jnp.dot(normed_ffn, w_gate, preferred_element_type=jnp.float32)
    up_proj = jnp.dot(normed_ffn, w_up, preferred_element_type=jnp.float32)
    act = (jax.nn.silu(gate) * up_proj).astype(jnp.bfloat16)
    layer_out = (
        hidden_state
        + lax.psum_scatter(
            jnp.dot(act, w_down, preferred_element_type=jnp.float32).astype(jnp.bfloat16),
            "tp",
            scatter_dimension=0,
            tiled=True,
        ).astype(jnp.float32)
    ).astype(jnp.bfloat16)
    grad_y = out_cotangent[0].astype(jnp.float32)
    grad_fb = lax.all_gather(grad_y.astype(jnp.bfloat16), "tp", axis=0, tiled=True)
    grad_down = contract_rows(act, grad_fb)
    grad_act = contract_cols(grad_fb, w_down)
    sigma = jax.nn.sigmoid(gate)
    grad_gate = (grad_act * up_proj * sigma * (1.0 + gate * (1.0 - sigma))).astype(jnp.bfloat16)
    grad_up = (grad_act * gate * sigma).astype(jnp.bfloat16)
    grad_gate_w = contract_rows(normed_ffn, grad_gate)
    grad_up_w = contract_rows(normed_ffn, grad_up)
    grad_nffn = lax.psum_scatter(
        (contract_cols(grad_gate, w_gate) + contract_cols(grad_up, w_up)).astype(jnp.bfloat16),
        "tp",
        scatter_dimension=0,
        tiled=True,
    ).astype(jnp.float32)
    norm_pull = jax.vjp(rms_norm, hidden_state, ffn_gain)[1]
    grad_state_norm, grad_ffn_gain = norm_pull(grad_nffn)
    grad_state = grad_y + grad_state_norm
    grad_sb = lax.all_gather(grad_state.astype(jnp.bfloat16), "tp", axis=0, tiled=True)
    grad_out_w = contract_rows(merged, grad_sb)
    grad_merged = contract_cols(grad_sb, w_out).astype(jnp.bfloat16)
    grad_att = grad_merged.reshape(ctx_rows, kv_heads, per_group, HD).transpose(1, 2, 0, 3).reshape(
        kv_heads, query_rows, HD
    ) * valid_rows[None, :, None].astype(jnp.bfloat16)
    delta = jnp.sum(grad_att.astype(jnp.float32) * attended, axis=2)
    all_keys, all_values = (
        lax.all_gather(rot_keys, "ctx", axis=0, tiled=True),
        lax.all_gather(values, "ctx", axis=0, tiled=True),
    )

    def back_block(step_num, state_in):
        grad_rows, grad_key_all, grad_value_all = state_in
        offset = step_num * ctx_rows
        key_blk = lax.dynamic_slice_in_dim(all_keys, offset, ctx_rows, 0)
        value_blk = lax.dynamic_slice_in_dim(all_values, offset, ctx_rows, 0)
        scores, allowed = scores_of(key_blk, offset)
        probs = jnp.where(allowed[None], jnp.exp(scores - log_total[:, :, None]), 0.0)
        grad_probs = jnp.einsum(
            "hrd,khd->hrk", grad_att, value_blk, preferred_element_type=jnp.float32
        )
        grad_scores = (probs * (grad_probs - delta[:, :, None])).astype(jnp.bfloat16)
        grad_rows = (
            grad_rows
            + jnp.einsum("hrk,khd->hrd", grad_scores, key_blk, preferred_element_type=jnp.float32)
            * score_scale
        )
        key_grad = (
            jnp.einsum("hrk,hrd->khd", grad_scores, query_mat, preferred_element_type=jnp.float32)
            * score_scale
        )
        value_grad = jnp.einsum(
            "hrk,hrd->khd", probs.astype(jnp.bfloat16), grad_att, preferred_element_type=jnp.float32
        )
        grad_key_all = lax.dynamic_update_slice_in_dim(grad_key_all, key_grad, offset, 0)
        grad_value_all = lax.dynamic_update_slice_in_dim(grad_value_all, value_grad, offset, 0)
        return (grad_rows, grad_key_all, grad_value_all)

    start_grads = (
        jnp.zeros((kv_heads, query_rows, HD), jnp.float32),
        jnp.zeros((ctx_rows * ctx_count, kv_heads, HD), jnp.float32),
        jnp.zeros((ctx_rows * ctx_count, kv_heads, HD), jnp.float32),
    )
    grad_rows, grad_key_all, grad_value_all = lax.fori_loop(0, ctx_count, back_block, start_grads)
    grad_rk, grad_vals = (
        lax.psum_scatter(
            grad_key_all.astype(jnp.bfloat16), "ctx", scatter_dimension=0, tiled=True
        ).astype(jnp.float32),
        lax.psum_scatter(
            grad_value_all.astype(jnp.bfloat16), "ctx", scatter_dimension=0, tiled=True
        ).astype(jnp.float32),
    )
    grad_rq = (
        grad_rows.reshape(kv_heads, per_group, ctx_rows, HD)
        .transpose(2, 0, 1, 3)
        .reshape(ctx_rows, q_heads, HD)
    )
    grad_queries = (
        unrotate(grad_rq, cosine, sine_part).astype(jnp.bfloat16).reshape(ctx_rows, q_heads * HD)
    )
    grad_keys = (
        unrotate(grad_rk, cosine, sine_part).astype(jnp.bfloat16).reshape(ctx_rows, kv_heads * HD)
    )
    grad_vals_low = grad_vals.astype(jnp.bfloat16).reshape(ctx_rows, kv_heads * HD)
    grad_query_w = contract_rows(normed, grad_queries)
    grad_key_w = contract_rows(normed, grad_keys)
    grad_value_w = contract_rows(normed, grad_vals_low)
    grad_normed = lax.psum_scatter(
        (
            contract_cols(grad_queries, w_query)
            + contract_cols(grad_keys, w_key)
            + contract_cols(grad_vals_low, w_value)
        ).astype(jnp.bfloat16),
        "tp",
        scatter_dimension=0,
        tiled=True,
    ).astype(jnp.float32)
    first_pull = jax.vjp(rms_norm, inputs, attn_gain)[1]
    grad_input_norm, grad_attn_gain = first_pull(grad_normed)
    input_grad = grad_state + grad_input_norm
    summed = (
        lax.psum_scatter(
            grad_query_w.astype(jnp.bfloat16), ("dp", "ctx"), scatter_dimension=0, tiled=True
        ).astype(jnp.float32),
        lax.psum_scatter(
            grad_key_w.astype(jnp.bfloat16), ("dp", "ctx"), scatter_dimension=0, tiled=True
        ).astype(jnp.float32),
        lax.psum_scatter(
            grad_value_w.astype(jnp.bfloat16), ("dp", "ctx"), scatter_dimension=0, tiled=True
        ).astype(jnp.float32),
        lax.psum_scatter(
            grad_out_w.astype(jnp.bfloat16), ("dp", "ctx"), scatter_dimension=1, tiled=True
        ).astype(jnp.float32),
        lax.psum_scatter(
            grad_gate_w.astype(jnp.bfloat16), ("dp", "ctx"), scatter_dimension=0, tiled=True
        ).astype(jnp.float32),
        lax.psum_scatter(
            grad_up_w.astype(jnp.bfloat16), ("dp", "ctx"), scatter_dimension=0, tiled=True
        ).astype(jnp.float32),
        lax.psum_scatter(
            grad_down.astype(jnp.bfloat16), ("dp", "ctx"), scatter_dimension=1, tiled=True
        ).astype(jnp.float32),
    )
    gains = lax.psum((grad_attn_gain, grad_ffn_gain), ("dp", "ctx", "tp"))
    return (
        layer_out[None],
        input_grad[None],
        gains[0],
        summed[0],
        summed[1],
        summed[2],
        summed[3],
        gains[1],
        summed[4],
        summed[5],
        summed[6],
    )


def solution(mesh):
    placed = (
        P("dp", ("ctx", "tp"), None),
        P(),
        P(None, "tp"),
        P(None, "tp"),
        P(None, "tp"),
        P("tp", None),
        P(),
        P(None, "tp"),
        P(None, "tp"),
        P("tp", None),
        P("dp", ("ctx", "tp"), None),
        P("dp", None),
    )
    return jax.shard_map(
        per_device,
        mesh=mesh,
        in_specs=placed,
        out_specs=(
            P("dp", ("ctx", "tp"), None),
            P("dp", ("ctx", "tp"), None),
            P(),
            P(("dp", "ctx"), "tp"),
            P(("dp", "ctx"), "tp"),
            P(("dp", "ctx"), "tp"),
            P("tp", ("dp", "ctx")),
            P(),
            P(("dp", "ctx"), "tp"),
            P(("dp", "ctx"), "tp"),
            P("tp", ("dp", "ctx")),
        ),
        check_vma=False,
    )
```

profile of v0, /device:TPU:0, one launch (start us, length us, event | category | flops | bytes accessed | tf_op | source)
XLA Modules:
  0.0 1209.5 jit_solution(17943840820172486991)
XLA Ops:
  14.7 22.5 %all-gather.6.cloned.1.call-done = bf16[512,2048]{1,0:T(8,128)(2,1)} async-done(((bf16[128,2048]{1,0:T(8,128)(2,1)}), bf16[512,2048]{1,0:T(8,128)(2,1)}) %all-gather.6.cloned.1.call-update) | async-done | bytes 2097168 | tf_op jit(solution)/shard_map/all_gather | solution.py:126
  40.0 16.1 %all_gather.21 = bf16[2048,2,64]{0,2,1:T(8,128)(2,1)S(1)} all-gather(bf16[512,2,64]{0,2,1:T(8,128)(2,1)S(1)} %pad_maximum_fusion.1), channel_id=1, replica_groups=mesh['dp'=2,'ctx'=4,'tp'=4] {'ctx'}, dimensions={0}, use_global_device_ids=true | all-gather | bytes 655360 | tf_op jit(solution)/shard_map/all_gather | solution.py:174
  56.9 16.8 %all_gather.22 = bf16[2048,2,64]{0,2,1:T(8,128)(2,1)} all-gather(bf16[512,2,64]{0,2,1:T(8,128)(2,1)S(1)} %bitcast.235), channel_id=1, replica_groups=mesh['dp'=2,'ctx'=4,'tp'=4] {'ctx'}, dimensions={0}, use_global_device_ids=true | all-gather | bytes 655360 | tf_op jit(solution)/shard_map/all_gather | solution.py:175
  78.1 41.1 %while.42 = (s32[]{:T(128)}, f32[2,2048]{1,0:T(2,128)S(1)}, f32[2,2048]{1,0:T(2,128)S(1)}, f32[2,2048,64]{1,2,0:T(8,128)}, s32[1,8]{1,0:T(1,128)S(1)}, /*index=5...) while((s32[]{:T(128)}, f32[2,2048]{1,0:T(2,128)S(1)}, ...), condition=%wide.region_8.9_spmd.clone, body=%wide.region_4.8_spmd.clone.sunk | while | flops 568116736 | bytes 40974632 | solution.py:184
  128.7 31.8 %reduce-scatter.14.cloned.1.call-done = bf16[128,2048]{1,0:T(8,128)(2,1)} async-done(((bf16[512,2048]{1,0:T(8,128)(2,1)}), bf16[128,2048]{1,0:T(8,128)(2,1)}) %reduce-scatter.14.cloned.1.call-update) | async-done | bytes 524304 | tf_op jit(solution)/shard_map/reduce_scatter | solution.py:193
  164.7 22.0 %all-gather.8.cloned.1.call-done = bf16[512,2048]{1,0:T(8,128)(2,1)} async-done(((bf16[128,2048]{1,0:T(8,128)(2,1)}), bf16[512,2048]{1,0:T(8,128)(2,1)}) %all-gather.8.cloned.1.call-update) | async-done | bytes 2097168 | tf_op jit(solution)/shard_map/all_gather | solution.py:200
  186.7 10.7 fusion.93
  197.3 9.3 fusion.92
  210.8 11.8 multiply_convert_fusion
  231.1 9.5 add_convert_fusion.1
  240.8 31.3 %reduce-scatter.18.cloned.1.call-done = bf16[128,2048]{1,0:T(8,128)(2,1)} async-done(((bf16[512,2048]{1,0:T(8,128)(2,1)}), bf16[128,2048]{1,0:T(8,128)(2,1)}) %reduce-scatter.18.cloned.1.call-update) | async-done | bytes 524304 | tf_op jit(solution)/shard_map/reduce_scatter | solution.py:222
  276.9 22.6 %all-gather.10.cloned.1.call-done = bf16[512,2048]{1,0:T(8,128)(2,1)} async-done(((bf16[128,2048]{1,0:T(8,128)(2,1)}), bf16[512,2048]{1,0:T(8,128)(2,1)}) %all-gather.10.cloned.1.call-update) | async-done | bytes 2097168 | tf_op jit(solution)/shard_map/all_gather | solution.py:231
  305.2 55.6 %while.43 = (s32[]{:T(128)}, f32[2,2048,64]{1,2,0:T(8,128)S(1)}, bf16[2048,2,64]{0,2,1:T(8,128)(2,1)}, bf16[2048,2,64]{0,2,1:T(8,128)(2,1)}, s32[1,8]{1,0:T(1,12...) while((s32[]{:T(128)}, f32[2,2048,64]{1,2,0:T(8,128)S(1)}, ...), condition=%wide.region_17.18_spmd.clone, body=%wide.region_15.17_spmd.clone.sunk | while | flops 1371371008 | bytes 58718652 | solution.py:275
  361.6 21.0 %reduce-scatter.20.cloned.1.call-done = bf16[512,2,64]{0,2,1:T(8,128)(2,1)} async-done(((bf16[2048,2,64]{0,2,1:T(8,128)(2,1)}), bf16[512,2,64]{0,2,1:T(8,128)(2,1)}) %reduce-scatter.20.cloned.1.call-update) | async-done | bytes 131088 | tf_op jit(solution)/shard_map/reduce_scatter | solution.py:277
  385.3 20.0 %reduce-scatter.22.cloned.1.call-done = bf16[512,2,64]{0,2,1:T(8,128)(2,1)} async-done(((bf16[2048,2,64]{0,2,1:T(8,128)(2,1)}), bf16[512,2,64]{0,2,1:T(8,128)(2,1)}) %reduce-scatter.22.cloned.1.call-update) | async-done | bytes 131088 | tf_op jit(solution)/shard_map/reduce_scatter | solution.py:280
  425.0 10.1 convolution_convert_fusion.5
  471.0 63.6 %reduce-scatter.30.cloned.1.call-done = bf16[256,128]{1,0:T(8,128)(2,1)} async-done(((bf16[2048,128]{1,0:T(8,128)(2,1)}), bf16[256,128]{1,0:T(8,128)(2,1)}) %reduce-scatter.30.cloned.1.call-update) | async-done | bytes 65552 | tf_op jit(solution)/shard_map/reduce_scatter | solution.py:319
  536.1 69.2 %reduce-scatter.32.cloned.1.call-done = bf16[512,256]{1,0:T(8,128)(2,1)} async-done(((bf16[512,2048]{1,0:T(8,128)(2,1)}), bf16[512,256]{1,0:T(8,128)(2,1)}) %reduce-scatter.32.cloned.1.call-update) | async-done | bytes 262160 | tf_op jit(solution)/shard_map/reduce_scatter | solution.py:322
  607.0 68.5 %reduce-scatter.26.cloned.1.call-done = bf16[256,512]{1,0:T(8,128)(2,1)} async-done(((bf16[2048,512]{1,0:T(8,128)(2,1)}), bf16[256,512]{1,0:T(8,128)(2,1)}) %reduce-scatter.26.cloned.1.call-update) | async-done | bytes 262160 | tf_op jit(solution)/shard_map/reduce_scatter | solution.py:313
  677.3 31.7 %reduce-scatter.24.cloned.1.call-done = bf16[128,2048]{1,0:T(8,128)(2,1)} async-done(((bf16[512,2048]{1,0:T(8,128)(2,1)}), bf16[128,2048]{1,0:T(8,128)(2,1)}) %reduce-scatter.24.cloned.1.call-update) | async-done | bytes 524304 | tf_op jit(solution)/shard_map/reduce_scatter | solution.py:299
  710.6 39.5 %all-reduce = (f32[2048]{0:T(1024)}, f32[2048]{0:T(1024)}) all-reduce(f32[2048]{0:T(1024)S(1)} %get-tuple-element.750, f32[2048]{0:T(1024)S(1)} %copy-done.32), channel_id=1, replica_groups=mesh['dp'=2,'ctx'=4,'tp'=4] {'dp','ctx','tp'}, use_global_device_ids=true, to_apply=%region_23.24 | all-reduce | flops 4096 | bytes 32768 | tf_op jit(solution)/shard_map/psum | solution.py:335
  753.8 142.7 %reduce-scatter.38.cloned.1.call-done = bf16[2048,256]{1,0:T(8,128)(2,1)} async-done(((bf16[2048,2048]{1,0:T(8,128)(2,1)}), bf16[2048,256]{1,0:T(8,128)(2,1)}) %reduce-scatter.38.cloned.1.call-update) | async-done | bytes 1048592 | tf_op jit(solution)/shard_map/reduce_scatter | solution.py:331
  899.2 149.3 %reduce-scatter.36.cloned.1.call-done = bf16[256,2048]{1,0:T(8,128)(2,1)} async-done(((bf16[2048,2048]{1,0:T(8,128)(2,1)}), bf16[256,2048]{1,0:T(8,128)(2,1)}) %reduce-scatter.36.cloned.1.call-update) | async-done | bytes 1048592 | tf_op jit(solution)/shard_map/reduce_scatter | solution.py:328
  1051.3 148.8 %reduce-scatter.34.cloned.1.call-done = bf16[256,2048]{1,0:T(8,128)(2,1)} async-done(((bf16[2048,2048]{1,0:T(8,128)(2,1)}), bf16[256,2048]{1,0:T(8,128)(2,1)}) %reduce-scatter.34.cloned.1.call-update) | async-done | bytes 1048592 | tf_op jit(solution)/shard_map/reduce_scatter | solution.py:325
  (340 shorter events, 225.3 us)
Async XLA Ops:
  7.2 30.1 %all-gather.6.cloned.1.call-start = ((), (), s32[]{:S(2)}) async-start(), calls=%async_computation.13 | async-start | bytes 2621440 | tf_op jit(solution)/shard_map/all_gather | solution.py:126
  11.8 148.7 %reduce-scatter.14.cloned.1.call-start = ((), (), s32[]{:S(2)}) async-start(), calls=%async_computation.14 | async-start | bytes 2621440 | tf_op jit(solution)/shard_map/reduce_scatter | solution.py:193
  128.6 58.0 %all-gather.8.cloned.1.call-start = ((), (), s32[]{:S(2)}) async-start(), calls=%async_computation.15 | async-start | bytes 2621440 | tf_op jit(solution)/shard_map/all_gather | solution.py:200
  163.9 46.9 %all-gather.12.cloned.1.call-start = ((), (), s32[]{:S(2)}) async-start(), calls=%async_computation.29 | async-start | bytes 2621440 | tf_op jit(solution)/shard_map/all_gather | solution.py:214
  164.5 107.7 %reduce-scatter.18.cloned.1.call-start = ((), (), s32[]{:S(2)}) async-start(), calls=%async_computation.17 | async-start | bytes 2621440 | tf_op jit(solution)/shard_map/reduce_scatter | solution.py:222
  240.6 58.9 %all-gather.10.cloned.1.call-start = ((), (), s32[]{:S(2)}) async-start(), calls=%async_computation.18 | async-start | bytes 2621440 | tf_op jit(solution)/shard_map/all_gather | solution.py:231
  276.8 105.9 %reduce-scatter.20.cloned.1.call-start = ((), (), s32[]{:S(2)}) async-start(), calls=%async_computation.19 | async-start | bytes 655360 | tf_op jit(solution)/shard_map/reduce_scatter | solution.py:277
  360.8 44.5 %reduce-scatter.22.cloned.1.call-start = ((), (), s32[]{:S(2)}) async-start(), calls=%async_computation.20 | async-start | bytes 655360 | tf_op jit(solution)/shard_map/reduce_scatter | solution.py:280
  361.6 107.9 %reduce-scatter.28.cloned.1.call-start = ((), (), s32[]{:S(2)}) async-start(), calls=%async_computation.23 | async-start | bytes 589824 | tf_op jit(solution)/shard_map/reduce_scatter | solution.py:316
  385.2 149.3 %reduce-scatter.30.cloned.1.call-start = ((), (), s32[]{:S(2)}) async-start(), calls=%async_computation.24 | async-start | bytes 589824 | tf_op jit(solution)/shard_map/reduce_scatter | solution.py:319
  407.8 197.4 %reduce-scatter.32.cloned.1.call-start = ((), (), s32[]{:S(2)}) async-start(), calls=%async_computation.25 | async-start | bytes 2359296 | tf_op jit(solution)/shard_map/reduce_scatter | solution.py:322
  412.3 263.2 %reduce-scatter.26.cloned.1.call-start = ((), (), s32[]{:S(2)}) async-start(), calls=%async_computation.22 | async-start | bytes 2359296 | tf_op jit(solution)/shard_map/reduce_scatter | solution.py:313
  418.8 290.2 %reduce-scatter.24.cloned.1.call-start = ((), (), s32[]{:S(2)}) async-start(), calls=%async_computation.21 | async-start | bytes 2621440 | tf_op jit(solution)/shard_map/reduce_scatter | solution.py:299
  425.0 325.1 %reduce-scatter.16.cloned.1.call-start = ((), (), s32[]{:S(2)}) async-start(), calls=%async_computation.16 | async-start | bytes 2621440 | tf_op jit(solution)/shard_map/reduce_scatter | solution.py:206
  435.1 461.4 %reduce-scatter.38.cloned.1.call-start = ((), (), s32[]{:S(2)}) async-start(), calls=%async_computation.28 | async-start | bytes 9437184 | tf_op jit(solution)/shard_map/reduce_scatter | solution.py:331
  443.7 604.8 %reduce-scatter.36.cloned.1.call-start = ((), (), s32[]{:S(2)}) async-start(), calls=%async_computation.27 | async-start | bytes 9437184 | tf_op jit(solution)/shard_map/reduce_scatter | solution.py:328
  453.6 746.4 %reduce-scatter.34.cloned.1.call-start = ((), (), s32[]{:S(2)}) async-start(), calls=%async_computation.26 | async-start | bytes 9437184 | tf_op jit(solution)/shard_map/reduce_scatter | solution.py:325
  462.1 248.5 %copy-start.32 = (f32[2048]{0:T(1024)S(1)}, f32[2048]{0:T(1024)}, u32[]{:S(2)}) copy-start(f32[2048]{0:T(1024)} %get-tuple-element.748) | copy-start | bytes 24580
  462.1 288.0 %copy-start.40 = (f32[128]{0:T(128)S(1)}, f32[128]{0:T(128)}, u32[]{:S(2)}) copy-start(f32[128]{0:T(128)} %copy-done.39) | copy-start | bytes 1540
  462.1 288.0 %copy-start.9 = (bf16[128,2048]{1,0:T(8,128)(2,1)S(1)}, bf16[128,2048]{1,0:T(8,128)(2,1)}, u32[]{:S(2)}) copy-start(bf16[128,2048]{1,0:T(8,128)(2,1)} %reduce-scatter.14.cloned.1.call-done) | copy-start | bytes 1572868
  462.1 288.0 %copy-start.30 = (f32[2048]{0:T(1024)S(1)}, f32[2048]{0:T(1024)}, u32[]{:S(2)}) copy-start(f32[2048]{0:T(1024)} %param.23) | copy-start | bytes 24580
  462.1 288.0 %copy-start.34 = (f32[128]{0:T(128)S(1)}, f32[128]{0:T(128)}, u32[]{:S(2)}) copy-start(f32[128]{0:T(128)} %copy-done.33) | copy-start | bytes 1540
  462.1 288.0 %copy-start.38 = (f32[128]{0:T(128)S(1)}, f32[128]{0:T(128)}, u32[]{:S(2)}) copy-start(f32[128]{0:T(128)} %copy-done.37) | copy-start | bytes 1540
  750.2 452.7 %copy-start.1 = (bf16[512,2048]{1,0:T(8,128)(2,1)S(1)}, bf16[512,2048]{1,0:T(8,128)(2,1)}, u32[]{:S(2)}) copy-start(bf16[512,2048]{1,0:T(8,128)(2,1)} %param.22) | copy-start | bytes 6291460
  (63 other events, 1732.1 us)
Sparse Core Ops, SparseCore 0:
  11.9 25.2 all-gather.5
  128.8 31.7 reduce-scatter.13
  164.0 22.5 all-gather.7
  188.1 22.5 all-gather.11
  240.7 31.4 reduce-scatter.17
  276.9 22.5 all-gather.9
  360.9 21.6 reduce-scatter.19
  385.5 19.7 reduce-scatter.21
  409.2 60.2 reduce-scatter.27
  473.6 60.8 reduce-scatter.29
  538.1 67.0 reduce-scatter.31
  608.6 66.7 reduce-scatter.25
  678.6 30.3 reduce-scatter.23
  712.1 31.5 reduce-scatter.15
  747.1 149.3 reduce-scatter.37
  900.4 148.0 reduce-scatter.35
  1052.0 148.0 reduce-scatter.33
where the time goes:
time: 1210 us
  waiting for transfers between devices  858 us (71%)
  matrix products  186 us (15%)
  blocking collectives  72.3 us (6%)
  other arithmetic  57.8 us (5%)
  local copies, waits for them, and re-layouts  18 us (1%)
  between operations  14.7 us (1%)
    reduce_scatter x1, waiting for transfers between devices, per_device(): lax.psum_scatter(grad_up_w.astype(jnp.bfloat16), ('dp', 'ctx'), scatter_d...  149 us
    reduce_scatter x1, waiting for transfers between devices, per_device(): lax.psum_scatter(grad_gate_w.astype(jnp.bfloat16), ('dp', 'ctx'), scatter...  149 us
    reduce_scatter x1, waiting for transfers between devices, per_device(): lax.psum_scatter(grad_down.astype(jnp.bfloat16), ('dp', 'ctx'), scatter_d...  143 us
    reduce_scatter x1, waiting for transfers between devices, per_device(): lax.psum_scatter(grad_out_w.astype(jnp.bfloat16), ('dp', 'ctx'), scatter_...  69.2 us
    reduce_scatter x1, waiting for transfers between devices, per_device(): lax.psum_scatter(grad_query_w.astype(jnp.bfloat16), ('dp', 'ctx'), scatte...  68.5 us
    reduce_scatter x1, waiting for transfers between devices, per_device(): lax.psum_scatter(grad_value_w.astype(jnp.bfloat16), ('dp', 'ctx'), scatte...  63.6 us
    psum x1, blocking collectives, per_device(): gains = lax.psum((grad_attn_gain, grad_ffn_gain), ('dp', 'ctx', 'tp'))  39.5 us
    dot_general x7, matrix products, contract_cols(): lax.dot_general(left, right, (((1,), (1,)), ((), ())), preferred_element_...  38.4 us
  transfers between devices with their start and end apart: 17, of which 16 were waited for; matrix products, arithmetic and copies ran while one was open for 8% of the time, Pallas kernels for 0%

commit v1 on v0

v1 whole, which is shorter than its diff:
```python
import math

import jax
import jax.numpy as jnp
import numpy as np
from jax import lax
from jax.sharding import PartitionSpec as P

HD = 64


EPSILON = 1e-05
NEGATIVE = -1e30
START_MAX = -1e20
ROPE_THETA = 500000.0


def rope_table(head_size):
    base_freq = np.array(
        [ROPE_THETA ** (-2.0 * index / head_size) for index in range(head_size // 2)]
    )
    wavelength = 2.0 * math.pi / base_freq
    blend = (8192.0 / wavelength - 1.0) / 3.0
    middle = (1.0 - blend) * base_freq / 32.0 + blend * base_freq
    return np.where(
        wavelength > 8192.0, base_freq / 32.0, np.where(wavelength < 2048.0, base_freq, middle)
    )


def block_positions(owner, within, ctx_rows, ctx_count):
    half_rows = ctx_rows // 2
    piece_num = jnp.where(within < half_rows, owner, 2 * ctx_count - 1 - owner)
    return (piece_num * half_rows + within % half_rows).astype(jnp.int32)


def doc_segments(positions, doc_row):
    ends = jnp.cumsum(doc_row)
    return jnp.sum((positions[:, None] >= ends[None, :]).astype(jnp.int32), axis=1)


def rms_norm(values_in, gain_vec):
    return (
        values_in
        * lax.rsqrt(jnp.mean(values_in * values_in, axis=-1, keepdims=True) + EPSILON)
        * gain_vec
    )


def rotate(values_in, cosine, sine_part):
    halfway = values_in.shape[-1] // 2
    first_half = values_in[..., :halfway]
    second_half = values_in[..., halfway:]
    return jnp.concatenate(
        [
            first_half * cosine - second_half * sine_part,
            second_half * cosine + first_half * sine_part,
        ],
        axis=-1,
    )


def unrotate(values_in, cosine, sine_part):
    halfway = values_in.shape[-1] // 2
    first_half = values_in[..., :halfway]
    second_half = values_in[..., halfway:]
    return jnp.concatenate(
        [
            first_half * cosine + second_half * sine_part,
            second_half * cosine - first_half * sine_part,
        ],
        axis=-1,
    )


def contract_rows(left, right):
    return lax.dot_general(
        left, right, (((0,), (0,)), ((), ())), preferred_element_type=jnp.float32
    )


def contract_cols(left, right):
    return lax.dot_general(
        left, right, (((1,), (1,)), ((), ())), preferred_element_type=jnp.float32
    )


def matmul(left, right):
    return jnp.dot(left, right, preferred_element_type=jnp.float32)


def flip(values_in, axis, mask):
    count = lax.axis_size(axis)
    return lax.ppermute(values_in, axis, [(i, i ^ mask) for i in range(count)])


def tp_gather(shard):
    count = lax.axis_size("tp")
    parts = {0: shard}
    mask = 2
    while mask < count:
        parts.update({j ^ mask: flip(part, "tp", mask) for j, part in parts.items()})
        mask *= 2
    parts.update({j ^ 1: flip(part, "tp", 1) for j, part in parts.items()})
    return jnp.concatenate([parts[j] for j in range(count)], axis=0)


def tp_scatter(near, far):
    count = lax.axis_size("tp")
    rows = 2 * near.shape[0] // count
    blocks = {}
    for first, terms in ((count // 2, far), (0, near)):
        terms = terms.astype(jnp.bfloat16)
        for j in range(0, count // 2, 2):
            kept, sent = terms[j * rows : (j + 1) * rows], terms[(j + 1) * rows : (j + 2) * rows]
            blocks[first + j] = kept.astype(jnp.float32) + flip(sent, "tp", 1).astype(jnp.float32)
    mask = count // 2
    while mask > 1:
        for j in range(0, mask, 2):
            sent = flip(blocks[j + mask].astype(jnp.bfloat16), "tp", mask)
            blocks[j] = blocks[j] + sent.astype(jnp.float32)
        mask //= 2
    return blocks[0]


def line_scatter(terms, axis, dim):
    count = lax.axis_size(axis)
    rank = lax.axis_index(axis)
    size = terms.shape[dim] // count

    def chunk(index):
        index = jnp.clip(index, 0, count - 1)
        return lax.dynamic_slice_in_dim(terms, index * size, size, dim).astype(jnp.float32)

    up, down = None, None
    for step in range(1, count):
        up_term = chunk(count - step + rank)
        down_term = chunk(rank - count + step)
        if up is not None:
            up_term = up_term + up.astype(jnp.float32)
            down_term = down_term + down.astype(jnp.float32)
        up = lax.ppermute(
            up_term.astype(jnp.bfloat16), axis, [(i, i + 1) for i in range(step)]
        )
        down = lax.ppermute(
            down_term.astype(jnp.bfloat16),
            axis,
            [(count - 1 - i, count - 2 - i) for i in range(step)],
        )
    return chunk(rank) + up.astype(jnp.float32) + down.astype(jnp.float32)


def sum_everywhere(values_in):
    for axis in ("tp", "dp", "ctx"):
        mask = 1
        while mask < lax.axis_size(axis):
            values_in = values_in + flip(values_in, axis, mask)
            mask *= 2
    return values_in


def half_of(values_in, index):
    size = values_in.shape[1] // lax.axis_size("dp")
    return lax.dynamic_slice_in_dim(values_in, index * size, size, 1)


def wide_pair(shard, whole):
    me = lax.axis_index("dp")
    other = flip(half_of(shard, 1 - me), "dp", 1)
    return half_of(whole, me), tp_gather(other)


def weight_grad(narrow, wide, narrow_first):
    narrow_other = flip(narrow, "dp", 1)
    if narrow_first:
        terms = contract_rows(narrow, wide[0]) + contract_rows(narrow_other, wide[1])
        return line_scatter(terms.astype(jnp.bfloat16), "ctx", 1)
    terms = contract_rows(wide[0], narrow) + contract_rows(wide[1], narrow_other)
    return line_scatter(terms.astype(jnp.bfloat16), "ctx", 0)


def per_device(
    tokens,
    attn_gain,
    w_query,
    w_key,
    w_value,
    w_out,
    ffn_gain,
    w_gate,
    w_up,
    w_down,
    out_cotangent,
    doc_lengths,
):
    ctx_count = lax.axis_size("ctx")
    ctx_rank = lax.axis_index("ctx")
    tp_count = lax.axis_size("tp")
    tp_rows = tokens.shape[1]
    ctx_rows = tp_rows * tp_count
    near_rows = ctx_rows // 2
    kv_heads = w_key.shape[1] // HD
    q_heads = w_query.shape[1] // HD
    per_group = q_heads // kv_heads
    query_rows = per_group * ctx_rows
    score_scale = 1.0 / math.sqrt(HD)
    doc_row = doc_lengths[0]
    index = jnp.arange(ctx_rows, dtype=jnp.int32)
    within = (lax.axis_index("tp") ^ (index // tp_rows)) * tp_rows + index % tp_rows
    block_pos = [
        block_positions((ctx_rank + k) % ctx_count, within, ctx_rows, ctx_count)
        for k in range(ctx_count)
    ]
    block_seg = [doc_segments(pos, doc_row) for pos in block_pos]
    query_pos, query_seg = block_pos[0], block_seg[0]
    is_valid = (query_seg < doc_row.shape[0]).astype(jnp.float32)
    row_pos = jnp.tile(query_pos, per_group)
    row_seg = jnp.tile(query_seg, per_group)
    valid_rows = jnp.tile(is_valid, per_group)
    inv_freq = jnp.asarray(rope_table(HD), jnp.float32)
    angles = query_pos.astype(jnp.float32)[:, None] * inv_freq[None, :]
    cosine = jnp.cos(angles)[:, None, :]
    sine_part = jnp.sin(angles)[:, None, :]

    inputs = tokens[0].astype(jnp.float32)
    normed_local = rms_norm(inputs, attn_gain).astype(jnp.bfloat16)
    normed = tp_gather(normed_local)
    grad_fb_local = out_cotangent[0]
    grad_fb = tp_gather(grad_fb_local)
    grad_y = grad_fb_local.astype(jnp.float32)
    queries = matmul(normed, w_query).reshape(ctx_rows, q_heads, HD)
    keys_raw = matmul(normed, w_key).reshape(ctx_rows, kv_heads, HD)
    values = matmul(normed, w_value).astype(jnp.bfloat16)
    rot_queries = rotate(queries, cosine, sine_part).astype(jnp.bfloat16)
    rot_keys = (
        rotate(keys_raw, cosine, sine_part).astype(jnp.bfloat16).reshape(ctx_rows, kv_heads * HD)
    )
    query_mat = (
        rot_queries.reshape(ctx_rows, kv_heads, per_group, HD)
        .transpose(1, 2, 0, 3)
        .reshape(kv_heads, query_rows, HD)
    )
    packed = jnp.concatenate([rot_keys, values], axis=1)

    def shift(values_in, k):
        return lax.ppermute(
            values_in, "ctx", [((i + k) % ctx_count, i) for i in range(ctx_count)]
        )

    kv_blocks = [packed] + [shift(packed, k) for k in range(1, ctx_count)]
    kv_blocks = [blk.reshape(ctx_rows, 2, kv_heads, HD) for blk in kv_blocks]

    def scores_of(k):
        raw_scores = (
            jnp.einsum(
                "hrd,khd->hrk", query_mat, kv_blocks[k][:, 0], preferred_element_type=jnp.float32
            )
            * score_scale
        )
        allowed = (row_seg[:, None] == block_seg[k][None, :]) & (
            block_pos[k][None, :] <= row_pos[:, None]
        )
        return (jnp.where(allowed[None], raw_scores, NEGATIVE), allowed)

    row_max = jnp.full((kv_heads, query_rows), START_MAX, jnp.float32)
    row_sum = jnp.zeros((kv_heads, query_rows), jnp.float32)
    weighted = jnp.zeros((kv_heads, query_rows, HD), jnp.float32)
    for k in range(ctx_count):
        scores, allowed = scores_of(k)
        new_max = jnp.maximum(row_max, jnp.max(scores, axis=2))
        rescale = jnp.exp(row_max - new_max)
        expo = jnp.where(allowed[None], jnp.exp(scores - new_max[:, :, None]), 0.0)
        row_sum = row_sum * rescale + jnp.sum(expo, axis=2)
        weighted = weighted * rescale[:, :, None] + jnp.einsum(
            "hrk,khd->hrd",
            expo.astype(jnp.bfloat16),
            kv_blocks[k][:, 1],
            preferred_element_type=jnp.float32,
        )
        row_max = new_max
    attended = weighted / row_sum[:, :, None]
    log_total = row_max + jnp.log(row_sum)
    merged_heads = (attended * valid_rows[None, :, None]).astype(jnp.bfloat16)
    merged = (
        merged_heads.reshape(kv_heads, per_group, ctx_rows, HD)
        .transpose(2, 0, 1, 3)
        .reshape(ctx_rows, q_heads * HD)
    )
    hidden_state = inputs + tp_scatter(
        matmul(merged[:near_rows], w_out), matmul(merged[near_rows:], w_out)
    )
    normed_ffn_local = rms_norm(hidden_state, ffn_gain).astype(jnp.bfloat16)
    normed_ffn = tp_gather(normed_ffn_local)
    gate = matmul(normed_ffn, w_gate)
    up_proj = matmul(normed_ffn, w_up)
    act = (jax.nn.silu(gate) * up_proj).astype(jnp.bfloat16)
    wide_fb = wide_pair(grad_fb_local, grad_fb)
    grad_down = weight_grad(act, wide_fb, True)
    grad_act = contract_cols(grad_fb, w_down)
    sigma = jax.nn.sigmoid(gate)
    grad_gate = (grad_act * up_proj * sigma * (1.0 + gate * (1.0 - sigma))).astype(jnp.bfloat16)
    grad_up = (grad_act * gate * sigma).astype(jnp.bfloat16)
    wide_nffn = wide_pair(normed_ffn_local, normed_ffn)
    grad_gate_w = weight_grad(grad_gate, wide_nffn, False)
    grad_up_w = weight_grad(grad_up, wide_nffn, False)

    def nffn_terms(rows):
        return contract_cols(grad_gate[rows], w_gate) + contract_cols(grad_up[rows], w_up)

    near, far = slice(0, near_rows), slice(near_rows, ctx_rows)
    grad_nffn = tp_scatter(nffn_terms(near), nffn_terms(far))
    grad_state_norm, grad_ffn_gain = jax.vjp(rms_norm, hidden_state, ffn_gain)[1](grad_nffn)
    grad_state = grad_y + grad_state_norm
    grad_sb_local = grad_state.astype(jnp.bfloat16)
    grad_sb = tp_gather(grad_sb_local)
    grad_out_w = weight_grad(merged, wide_pair(grad_sb_local, grad_sb), True)
    layer_out = (
        hidden_state + tp_scatter(matmul(act[near], w_down), matmul(act[far], w_down))
    ).astype(jnp.bfloat16)
    grad_merged = contract_cols(grad_sb, w_out).astype(jnp.bfloat16)
    grad_att = grad_merged.reshape(ctx_rows, kv_heads, per_group, HD).transpose(1, 2, 0, 3).reshape(
        kv_heads, query_rows, HD
    ) * valid_rows[None, :, None].astype(jnp.bfloat16)
    delta = jnp.sum(grad_att.astype(jnp.float32) * attended, axis=2)

    grad_rows = jnp.zeros((kv_heads, query_rows, HD), jnp.float32)
    kv_grad = jnp.zeros((ctx_rows, 2, kv_heads, HD), jnp.float32)
    for k in reversed(range(ctx_count)):
        scores, allowed = scores_of(k)
        probs = jnp.where(allowed[None], jnp.exp(scores - log_total[:, :, None]), 0.0)
        grad_probs = jnp.einsum(
            "hrd,khd->hrk", grad_att, kv_blocks[k][:, 1], preferred_element_type=jnp.float32
        )
        grad_scores = (probs * (grad_probs - delta[:, :, None])).astype(jnp.bfloat16)
        grad_rows = (
            grad_rows
            + jnp.einsum(
                "hrk,khd->hrd",
                grad_scores,
                kv_blocks[k][:, 0],
                preferred_element_type=jnp.float32,
            )
            * score_scale
        )
        key_grad = (
            jnp.einsum("hrk,hrd->khd", grad_scores, query_mat, preferred_element_type=jnp.float32)
            * score_scale
        )
        value_grad = jnp.einsum(
            "hrk,hrd->khd", probs.astype(jnp.bfloat16), grad_att, preferred_element_type=jnp.float32
        )
        block_grad = jnp.stack([key_grad, value_grad], axis=1)
        if k:
            block_grad = lax.ppermute(
                block_grad.astype(jnp.bfloat16).reshape(ctx_rows, 2 * kv_heads * HD),
                "ctx",
                [(i, (i + k) % ctx_count) for i in range(ctx_count)],
            ).reshape(ctx_rows, 2, kv_heads, HD).astype(jnp.float32)
        kv_grad = kv_grad + block_grad
    grad_rk, grad_vals = kv_grad[:, 0], kv_grad[:, 1]
    grad_rq = (
        grad_rows.reshape(kv_heads, per_group, ctx_rows, HD)
        .transpose(2, 0, 1, 3)
        .reshape(ctx_rows, q_heads, HD)
    )
    grad_queries = (
        unrotate(grad_rq, cosine, sine_part).astype(jnp.bfloat16).reshape(ctx_rows, q_heads * HD)
    )
    grad_keys = (
        unrotate(grad_rk, cosine, sine_part).astype(jnp.bfloat16).reshape(ctx_rows, kv_heads * HD)
    )
    grad_vals_low = grad_vals.astype(jnp.bfloat16).reshape(ctx_rows, kv_heads * HD)
    grad_qkv = jnp.concatenate([grad_queries, grad_keys, grad_vals_low], axis=1)
    grad_qkv_w = weight_grad(grad_qkv, wide_pair(normed_local, normed), False)
    q_width, kv_width = q_heads * HD, kv_heads * HD

    def normed_terms(rows):
        return (
            contract_cols(grad_queries[rows], w_query)
            + contract_cols(grad_keys[rows], w_key)
            + contract_cols(grad_vals_low[rows], w_value)
        )

    grad_normed = tp_scatter(normed_terms(near), normed_terms(far))
    grad_input_norm, grad_attn_gain = jax.vjp(rms_norm, inputs, attn_gain)[1](grad_normed)
    input_grad = grad_state + grad_input_norm
    gains = sum_everywhere(jnp.stack([grad_attn_gain, grad_ffn_gain]))
    return (
        layer_out[None],
        input_grad[None],
        gains[0],
        grad_qkv_w[:, :q_width],
        grad_qkv_w[:, q_width : q_width + kv_width],
        grad_qkv_w[:, q_width + kv_width :],
        grad_out_w,
        gains[1],
        grad_gate_w,
        grad_up_w,
        grad_down,
    )


def solution(mesh):
    placed = (
        P("dp", ("ctx", "tp"), None),
        P(),
        P(None, "tp"),
        P(None, "tp"),
        P(None, "tp"),
        P("tp", None),
        P(),
        P(None, "tp"),
        P(None, "tp"),
        P("tp", None),
        P("dp", ("ctx", "tp"), None),
        P("dp", None),
    )
    return jax.shard_map(
        per_device,
        mesh=mesh,
        in_specs=placed,
        out_specs=(
            P("dp", ("ctx", "tp"), None),
            P("dp", ("ctx", "tp"), None),
            P(),
            P(("dp", "ctx"), "tp"),
            P(("dp", "ctx"), "tp"),
            P(("dp", "ctx"), "tp"),
            P("tp", ("dp", "ctx")),
            P(),
            P(("dp", "ctx"), "tp"),
            P(("dp", "ctx"), "tp"),
            P("tp", ("dp", "ctx")),
        ),
        check_vma=False,
    )
```

time: 1210 us -> 745 us (0.62)
  the two profiles are of different devices: /device:TPU:0 before, /device:TPU:18 now
where the time goes in v1:
time: 745 us; the launch traced here: 740 us
  waiting for transfers between devices  307 us (41%)
  matrix products  201 us (27%)
  starting transfers between devices  158 us (21%)
  other arithmetic  50.8 us (7%)
  local copies, waits for them, and re-layouts  20.5 us (3%)
    ppermute x15, waiting for transfers between devices, line_scatter(): lax.ppermute(down_term.astype(jnp.bfloat16), axis, [(count - 1 - i, count...  134 us
    ppermute x50, waiting for transfers between devices, flip(): return lax.ppermute(values_in, axis, [(i, i ^ mask) for i in range(count)])  124 us
    ppermute x15, starting transfers between devices, line_scatter(): lax.ppermute(down_term.astype(jnp.bfloat16), axis, [(count - 1 - i, count...  63.5 us
    ppermute x50, starting transfers between devices, flip(): return lax.ppermute(values_in, axis, [(i, i ^ mask) for i in range(count)])  61.8 us
    dot_general x10, matrix products, contract_rows(): lax.dot_general(left, right, (((0,), (0,)), ((), ())), preferred_element_...  46.1 us
    dot_general x12, matrix products, contract_cols(): lax.dot_general(left, right, (((1,), (1,)), ((), ())), preferred_element_...  41.1 us
    ppermute x15, waiting for transfers between devices, line_scatter(): lax.ppermute(up_term.astype(jnp.bfloat16), axis, [(i, i + 1) for i in ran...  37.6 us
    dot_general x9, matrix products, matmul(): return jnp.dot(left, right, preferred_element_type=jnp.float32)  29.3 us
  transfers between devices with their start and end apart: 86, of which 32 were waited for; matrix products, arithmetic and copies ran while one was open for 30% of the time, Pallas kernels for 0%

profile of v1, /device:TPU:18, one launch (start us, length us, event | category | flops | bytes accessed | tf_op | source)
XLA Modules:
  0.0 740.4 jit_solution(5153570973720876499)
XLA Ops:
  33.0 10.9 %collective-permute-done.5 = bf16[512,256]{0,1:T(8,128)(2,1)} collective-permute-done((bf16[512,256]{0,1:T(8,128)(2,1)}, bf16[512,256]{0,1:T(8,128)(2,1)}, u32[]{:S(2)}, u32[]{:S(2)}) %collective-permute-start.5) | collective-permute-done | bytes 262176 | tf_op jit(solution)/shard_map/ppermute | solution.py:245
  87.7 12.4 %collective-permute-done.8 = bf16[128,2048]{1,0:T(8,128)(2,1)S(1)} collective-permute-done((bf16[128,2048]{1,0:T(8,128)(2,1)S(1)}, bf16[128,2048]{1,0:T(8,128)(2,1)S(1)}, u32[]{:S(2)}, u32[]{:S(2)}) %collective-permute-start.8) | collective-permute-done | bytes 524320 | tf_op jit(solution)/shard_map/ppermute | solution.py:93
  103.6 13.1 %collective-permute-done.10 = bf16[128,2048]{1,0:T(8,128)(2,1)} collective-permute-done((bf16[128,2048]{1,0:T(8,128)(2,1)}, bf16[128,2048]{1,0:T(8,128)(2,1)}, u32[]{:S(2)}, u32[]{:S(2)}) %collective-permute-start.10) | collective-permute-done | bytes 524320 | tf_op jit(solution)/shard_map/ppermute | solution.py:93
  128.1 10.6 %fusion.204 = f32[512,2048]{1,0:T(8,128)} fusion(bf16[2048,2048]{1,0:T(8,128)(2,1)} %param.20, bf16[128,2048]{1,0:T(8,128)(2,1)} %collective-permute-done.11, bf16[128,2048]{1,0:T(8,128)(2,1)} %collective-permute-done.10, bf16[128,2048]{1,0:T(8,128)(2,1)} %collective-permute-done.9, bf16[128,2048]{1,0:T(8,128)(2,1)} %multiply_convert_fusion.7), kind=kOutput, calls=%fused_computation.341 | convolution fusion | flops 4303355904 | bytes 14680064 | tf_op jit(solution)/shard_map/dot_general | solution.py:88
  138.7 7.7 %fusion.203 = f32[512,2048]{1,0:T(8,128)} fusion(bf16[2048,2048]{1,0:T(8,128)(2,1)S(1)} %bitcast.263, bf16[128,2048]{1,0:T(8,128)(2,1)} %collective-permute-done.11, bf16[128,2048]{1,0:T(8,128)(2,1)} %collective-permute-done.10, bf16[128,2048]{1,0:T(8,128)(2,1)} %collective-permute-done.9, bf16[128,2048]{1,0:T(8,128)(2,1)} %multiply_convert_fusion.7), kind=kOutput, calls=%fused_computation.340 | convolution fusion | flops 4303355904 | bytes 14680064 | tf_op jit(solution)/shard_map/dot_general | solution.py:88
  146.5 14.4 %multiply_convert_fusion.4 = (bf16[512,2048]{1,0:T(8,128)(2,1)}, bf16[512,2048]{1,0:T(8,128)(2,1)}, bf16[512,2048]{1,0:T(8,128)(2,1)}) fusion(f32[512,2048]{1,0:T(8,128)} %fusion.204, f32[512,2048]{1,0:T(8,128)} %fusion.203, bf16[2048,2048]{1,0:T(8,128)(2,1)} %param.22, bf16[128,2048]{1,0:T(8,128)(2,1)S(1)} %collective-permute-done.17, ...), kind=kOutput, calls=%fused_computation.35 | convolution fusion | flops 4320133120 | bytes 25165824 | tf_op jit(solution)/shard_map/dot_general | solution.py:82
  167.1 7.5 %fusion.114 = f32[256,2048]{1,0:T(8,128)} fusion(bf16[2048,2048]{1,0:T(8,128)(2,1)} %param.20, bf16[512,2048]{1,0:T(8,128)(2,1)} %get-tuple-element.32), kind=kOutput, calls=%fused_computation.146 | convolution fusion | flops 2147483648 | bytes 11534336 | tf_op jit(solution)/shard_map/dot_general | solution.py:82
  198.9 9.9 %collective-permute-done.20 = bf16[128,2048]{1,0:T(8,128)(2,1)} collective-permute-done((bf16[128,2048]{1,0:T(8,128)(2,1)}, bf16[128,2048]{1,0:T(8,128)(2,1)}, u32[]{:S(2)}, u32[]{:S(2)}) %collective-permute-start.20) | collective-permute-done | bytes 524320 | tf_op jit(solution)/shard_map/ppermute | solution.py:93
  210.6 8.8 %collective-permute-done.14 = bf16[128,2048]{1,0:T(8,128)(2,1)} collective-permute-done((bf16[128,2048]{1,0:T(8,128)(2,1)}, bf16[128,2048]{1,0:T(8,128)(2,1)}, u32[]{:S(2)}, u32[]{:S(2)}) %collective-permute-start.14) | collective-permute-done | bytes 524320 | tf_op jit(solution)/shard_map/ppermute | solution.py:93
  263.3 7.1 fusion.97
  316.2 7.3 fusion.222
  330.8 15.4 %collective-permute-done.68 = bf16[512,2048]{1,0:T(8,128)(2,1)} collective-permute-done((bf16[512,2048]{1,0:T(8,128)(2,1)}, bf16[512,2048]{1,0:T(8,128)(2,1)}, u32[]{:S(2)}, u32[]{:S(2)}) %collective-permute-start.68) | collective-permute-done | bytes 2097184 | tf_op jit(solution)/shard_map/ppermute | solution.py:93
  346.1 7.3 fusion.223
  363.6 26.6 %collective-permute-done.75 = bf16[512,2048]{1,0:T(8,128)(2,1)S(1)} collective-permute-done((bf16[512,2048]{1,0:T(8,128)(2,1)S(1)}, bf16[512,2048]{1,0:T(8,128)(2,1)S(1)}, u32[]{:S(2)}, u32[]{:S(2)}) %collective-permute-start.75) | collective-permute-done | bytes 2097184 | tf_op jit(solution)/shard_map/ppermute | solution.py:93
  415.2 7.8 %collective-permute-done.52 = bf16[512,256]{1,0:T(8,128)(2,1)S(1)} collective-permute-done((bf16[512,256]{1,0:T(8,128)(2,1)S(1)}, bf16[512,256]{1,0:T(8,128)(2,1)S(1)}, u32[]{:S(2)}, u32[]{:S(2)}) %collective-permute-start.52) | collective-permute-done | bytes 262176 | tf_op jit(solution)/shard_map/ppermute | solution.py:141
  447.8 28.9 %collective-permute-start.56 = (bf16[512,256]{1,0:T(8,128)(2,1)S(1)}, bf16[512,256]{1,0:T(8,128)(2,1)S(1)}, u32[]{:S(2)}, u32[]{:S(2)}) collective-permute-start(bf16[512,256]{1,0:T(8,128)(2,1)S(1)} %add_convert_fusion.26), channel_id=1, source_target_pairs={{12,8},{8,4},{4,0},{13,9},{9,5},{5,1},{14,10},{10,6},{6,2},{15,11}... | collective-permute-start | bytes 786440 | tf_op jit(solution)/shard_map/ppermute | solution.py:144
  495.5 32.8 %collective-permute-start.34 = (f32[2,2048]{1,0:T(2,128)S(1)}, f32[2,2048]{1,0:T(2,128)S(1)}, u32[]{:S(2)}, u32[]{:S(2)}) collective-permute-start(f32[2,2048]{1,0:T(2,128)S(1)} %add.684), channel_id=1, source_target_pairs={{0,8},{4,12},{8,0},{12,4},{1,9},{5,13},{9,1},{13,5},{2,10},{6,14},... | collective-permute-start | bytes 49160 | tf_op jit(solution)/shard_map/ppermute | solution.py:93
  534.6 29.8 %collective-permute-done.41 = bf16[256,768]{1,0:T(8,128)(2,1)S(1)} collective-permute-done((bf16[256,768]{1,0:T(8,128)(2,1)S(1)}, bf16[256,768]{1,0:T(8,128)(2,1)S(1)}, u32[]{:S(2)}, u32[]{:S(2)}) %collective-permute-start.41) | collective-permute-done | bytes 393248 | tf_op jit(solution)/shard_map/ppermute | solution.py:141
  579.4 21.5 %collective-permute-done.44 = bf16[256,768]{1,0:T(8,128)(2,1)S(1)} collective-permute-done((bf16[256,768]{1,0:T(8,128)(2,1)S(1)}, bf16[256,768]{1,0:T(8,128)(2,1)S(1)}, u32[]{:S(2)}, u32[]{:S(2)}) %collective-permute-start.44) | collective-permute-done | bytes 393248 | tf_op jit(solution)/shard_map/ppermute | solution.py:144
  613.6 36.0 %collective-permute-done.45 = bf16[256,768]{1,0:T(8,128)(2,1)S(1)} collective-permute-done((bf16[256,768]{1,0:T(8,128)(2,1)S(1)}, bf16[256,768]{1,0:T(8,128)(2,1)S(1)}, u32[]{:S(2)}, u32[]{:S(2)}) %collective-permute-start.45) | collective-permute-done | bytes 393248 | tf_op jit(solution)/shard_map/ppermute | solution.py:144
  660.2 17.4 %collective-permute-done.84 = bf16[2048,256]{1,0:T(8,128)(2,1)S(1)} collective-permute-done((bf16[2048,256]{1,0:T(8,128)(2,1)S(1)}, bf16[2048,256]{1,0:T(8,128)(2,1)S(1)}, u32[]{:S(2)}, u32[]{:S(2)}) %collective-permute-start.84) | collective-permute-done | bytes 1048608 | tf_op jit(solution)/shard_map/ppermute | solution.py:144
  681.8 18.2 %collective-permute-done.67 = bf16[256,2048]{1,0:T(8,128)(2,1)S(1)} collective-permute-done((bf16[256,2048]{1,0:T(8,128)(2,1)S(1)}, bf16[256,2048]{1,0:T(8,128)(2,1)S(1)}, u32[]{:S(2)}, u32[]{:S(2)}) %collective-permute-start.67) | collective-permute-done | bytes 1048608 | tf_op jit(solution)/shard_map/ppermute | solution.py:144
  701.9 20.6 %collective-permute-done.74 = bf16[256,2048]{1,0:T(8,128)(2,1)S(1)} collective-permute-done((bf16[256,2048]{1,0:T(8,128)(2,1)S(1)}, bf16[256,2048]{1,0:T(8,128)(2,1)S(1)}, u32[]{:S(2)}, u32[]{:S(2)}) %collective-permute-start.74) | collective-permute-done | bytes 1048608 | tf_op jit(solution)/shard_map/ppermute | solution.py:144
  724.4 14.1 %collective-permute-done.85 = bf16[2048,256]{1,0:T(8,128)(2,1)S(1)} collective-permute-done((bf16[2048,256]{1,0:T(8,128)(2,1)S(1)}, bf16[2048,256]{1,0:T(8,128)(2,1)S(1)}, u32[]{:S(2)}, u32[]{:S(2)}) %collective-permute-start.85) | collective-permute-done | bytes 1048608 | tf_op jit(solution)/shard_map/ppermute | solution.py:144
  (525 shorter events, 351.0 us)
Async XLA Ops:
  126.6 71.8 %collective-permute-start.59 = (bf16[128,1024]{1,0:T(8,128)(2,1)}, bf16[128,1024]{1,0:T(8,128)(2,1)}, u32[]{:S(2)}, u32[]{:S(2)}) collective-permute-start(bf16[128,1024]{1,0:T(8,128)(2,1)} %collective-permute-done.57), channel_id=1, source_target_pairs={{0,2},{1,3},{2,0},{3,1},{4,6},{5,7},{6,4},{7,5},{8,10},{9,11},{10,... | collective-permute-start | bytes 786440 | tf_op jit(solution)/shard_map/ppermute | solution.py:93
  248.2 81.9 %collective-permute-start.37 = (bf16[128,1024]{1,0:T(8,128)(2,1)}, bf16[128,1024]{1,0:T(8,128)(2,1)}, u32[]{:S(2)}, u32[]{:S(2)}) collective-permute-start(bf16[128,1024]{1,0:T(8,128)(2,1)} %collective-permute-done.35), channel_id=1, source_target_pairs={{0,2},{1,3},{2,0},{3,1},{4,6},{5,7},{6,4},{7,5},{8,10},{9,11},{10,... | collective-permute-start | bytes 786440 | tf_op jit(solution)/shard_map/ppermute | solution.py:93
  249.8 185.5 %collective-permute-start.36 = (bf16[128,1024]{1,0:T(8,128)(2,1)}, bf16[128,1024]{1,0:T(8,128)(2,1)}, u32[]{:S(2)}, u32[]{:S(2)}) collective-permute-start(bf16[128,1024]{1,0:T(8,128)(2,1)} %collective-permute-done.35), channel_id=1, source_target_pairs={{0,1},{1,0},{2,3},{3,2},{4,5},{5,4},{6,7},{7,6},{8,9},{9,8},{10,11... | collective-permute-start | bytes 786440 | tf_op jit(solution)/shard_map/ppermute | solution.py:93
  249.8 80.5 %collective-permute-start.78 = (bf16[128,1024]{1,0:T(8,128)(2,1)}, bf16[128,1024]{1,0:T(8,128)(2,1)}, u32[]{:S(2)}, u32[]{:S(2)}) collective-permute-start(bf16[128,1024]{1,0:T(8,128)(2,1)} %collective-permute-done.76), channel_id=1, source_target_pairs={{0,2},{1,3},{2,0},{3,1},{4,6},{5,7},{6,4},{7,5},{8,10},{9,11},{10,... | collective-permute-start | bytes 786440 | tf_op jit(solution)/shard_map/ppermute | solution.py:93
  252.4 63.2 %collective-permute-start.61 = (bf16[512,2048]{1,0:T(8,128)(2,1)}, bf16[512,2048]{1,0:T(8,128)(2,1)}, u32[]{:S(2)}, u32[]{:S(2)}) collective-permute-start(bf16[512,2048]{1,0:T(8,128)(2,1)} %get-tuple-element.32), channel_id=1, source_target_pairs={{0,16},{16,0},{1,17},{17,1},{2,18},{18,2},{3,19},{19,3},{4,20},{20... | collective-permute-start | bytes 6291464 | tf_op jit(solution)/shard_map/ppermute | solution.py:93
  253.0 93.2 %collective-permute-start.68 = (bf16[512,2048]{1,0:T(8,128)(2,1)}, bf16[512,2048]{1,0:T(8,128)(2,1)}, u32[]{:S(2)}, u32[]{:S(2)}) collective-permute-start(bf16[512,2048]{1,0:T(8,128)(2,1)} %get-tuple-element.31), channel_id=1, source_target_pairs={{0,16},{16,0},{1,17},{17,1},{2,18},{18,2},{3,19},{19,3},{4,20},{20... | collective-permute-start | bytes 6291464 | tf_op jit(solution)/shard_map/ppermute | solution.py:93
  315.6 74.5 %collective-permute-start.75 = (bf16[512,2048]{1,0:T(8,128)(2,1)S(1)}, bf16[512,2048]{1,0:T(8,128)(2,1)S(1)}, u32[]{:S(2)}, u32[]{:S(2)}) collective-permute-start(bf16[512,2048]{1,0:T(8,128)(2,1)S(1)} %copy-done.82), channel_id=1, source_target_pairs={{0,16},{16,0},{1,17},{17,1},{2,18},{18,2},{3,19},{19,3},{4,20},{20... | collective-permute-start | bytes 6291464 | tf_op jit(solution)/shard_map/ppermute | solution.py:93
  330.3 105.7 %collective-permute-start.38 = (bf16[128,1024]{1,0:T(8,128)(2,1)}, bf16[128,1024]{1,0:T(8,128)(2,1)S(1)}, u32[]{:S(2)}, u32[]{:S(2)}) collective-permute-start(bf16[128,1024]{1,0:T(8,128)(2,1)} %collective-permute-done.37), channel_id=1, source_target_pairs={{0,1},{1,0},{2,3},{3,2},{4,5},{5,4},{6,7},{7,6},{8,9},{9,8},{10,11... | collective-permute-start | bytes 786440 | tf_op jit(solution)/shard_map/ppermute | solution.py:93
  360.3 44.2 %collective-permute-start.26 = (bf16[512,256]{0,1:T(8,128)(2,1)S(1)}, bf16[512,256]{0,1:T(8,128)(2,1)S(1)}, u32[]{:S(2)}, u32[]{:S(2)}) collective-permute-start(bf16[512,256]{0,1:T(8,128)(2,1)S(1)} %bitcast.243), channel_id=1, source_target_pairs={{0,4},{4,8},{8,12},{12,0},{1,5},{5,9},{9,13},{13,1},{2,6},{6,10},{... | collective-permute-start | bytes 786440 | tf_op jit(solution)/shard_map/ppermute | solution.py:353
  433.9 132.1 %collective-permute-start.65 = (bf16[256,2048]{1,0:T(8,128)(2,1)S(1)}, bf16[256,2048]{1,0:T(8,128)(2,1)S(1)}, u32[]{:S(2)}, u32[]{:S(2)}) collective-permute-start(bf16[256,2048]{1,0:T(8,128)(2,1)S(1)} %get-tuple-element.45), channel_id=1, source_target_pairs={{12,8},{13,9},{14,10},{15,11},{28,24},{29,25},{30,26},{31,27}} | collective-permute-start | bytes 3145736 | tf_op jit(solution)/shard_map/ppermute | solution.py:144
  436.0 43.3 %collective-permute-start.80 = (bf16[2048,256]{1,0:T(8,128)(2,1)S(1)}, bf16[2048,256]{1,0:T(8,128)(2,1)S(1)}, u32[]{:S(2)}, u32[]{:S(2)}) collective-permute-start(bf16[2048,256]{1,0:T(8,128)(2,1)S(1)} %get-tuple-element.36), channel_id=1, source_target_pairs={{0,4},{1,5},{2,6},{3,7},{16,20},{17,21},{18,22},{19,23}} | collective-permute-start | bytes 3145736 | tf_op jit(solution)/shard_map/ppermute | solution.py:141
  478.7 52.6 %collective-permute-start.40 = (bf16[256,768]{1,0:T(8,128)(2,1)S(1)}, bf16[256,768]{1,0:T(8,128)(2,1)S(1)}, u32[]{:S(2)}, u32[]{:S(2)}) collective-permute-start(bf16[256,768]{1,0:T(8,128)(2,1)S(1)} %get-tuple-element.48), channel_id=1, source_target_pairs={{0,4},{1,5},{2,6},{3,7},{16,20},{17,21},{18,22},{19,23}} | collective-permute-start | bytes 1179656 | tf_op jit(solution)/shard_map/ppermute | solution.py:141
  483.2 49.5 %collective-permute-start.43 = (bf16[256,768]{1,0:T(8,128)(2,1)S(1)}, bf16[256,768]{1,0:T(8,128)(2,1)S(1)}, u32[]{:S(2)}, u32[]{:S(2)}) collective-permute-start(bf16[256,768]{1,0:T(8,128)(2,1)S(1)} %get-tuple-element.49), channel_id=1, source_target_pairs={{12,8},{13,9},{14,10},{15,11},{28,24},{29,25},{30,26},{31,27}} | collective-permute-start | bytes 1179656 | tf_op jit(solution)/shard_map/ppermute | solution.py:144
  484.5 82.8 %collective-permute-start.63 = (bf16[256,2048]{1,0:T(8,128)(2,1)S(1)}, bf16[256,2048]{1,0:T(8,128)(2,1)S(1)}, u32[]{:S(2)}, u32[]{:S(2)}) collective-permute-start(bf16[256,2048]{1,0:T(8,128)(2,1)S(1)} %add_convert_fusion.15), channel_id=1, source_target_pairs={{0,4},{4,8},{1,5},{5,9},{2,6},{6,10},{3,7},{7,11},{16,20},{20,24},... | collective-permute-start | bytes 3145736 | tf_op jit(solution)/shard_map/ppermute | solution.py:141
  531.3 43.3 %collective-permute-start.70 = (bf16[256,2048]{1,0:T(8,128)(2,1)S(1)}, bf16[256,2048]{1,0:T(8,128)(2,1)S(1)}, u32[]{:S(2)}, u32[]{:S(2)}) collective-permute-start(bf16[256,2048]{1,0:T(8,128)(2,1)S(1)} %add_convert_fusion.11), channel_id=1, source_target_pairs={{0,4},{4,8},{1,5},{5,9},{2,6},{6,10},{3,7},{7,11},{16,20},{20,24},... | collective-permute-start | bytes 3145736 | tf_op jit(solution)/shard_map/ppermute | solution.py:141
  574.6 77.1 %collective-permute-start.66 = (bf16[256,2048]{1,0:T(8,128)(2,1)S(1)}, bf16[256,2048]{1,0:T(8,128)(2,1)S(1)}, u32[]{:S(2)}, u32[]{:S(2)}) collective-permute-start(bf16[256,2048]{1,0:T(8,128)(2,1)S(1)} %get-tuple-element.43), channel_id=1, source_target_pairs={{12,8},{8,4},{13,9},{9,5},{14,10},{10,6},{15,11},{11,7},{28,24},{2... | collective-permute-start | bytes 3145736 | tf_op jit(solution)/shard_map/ppermute | solution.py:144
  600.9 79.0 %collective-permute-start.64 = (bf16[256,2048]{1,0:T(8,128)(2,1)S(1)}, bf16[256,2048]{1,0:T(8,128)(2,1)S(1)}, u32[]{:S(2)}, u32[]{:S(2)}) collective-permute-start(bf16[256,2048]{1,0:T(8,128)(2,1)S(1)} %get-tuple-element.42), channel_id=1, source_target_pairs={{0,4},{4,8},{8,12},{1,5},{5,9},{9,13},{2,6},{6,10},{10,14},{3,7},{... | collective-permute-start | bytes 3145736 | tf_op jit(solution)/shard_map/ppermute | solution.py:141
  602.9 52.7 %collective-permute-start.73 = (bf16[256,2048]{1,0:T(8,128)(2,1)S(1)}, bf16[256,2048]{1,0:T(8,128)(2,1)S(1)}, u32[]{:S(2)}, u32[]{:S(2)}) collective-permute-start(bf16[256,2048]{1,0:T(8,128)(2,1)S(1)} %get-tuple-element.39), channel_id=1, source_target_pairs={{12,8},{8,4},{13,9},{9,5},{14,10},{10,6},{15,11},{11,7},{28,24},{2... | collective-permute-start | bytes 3145736 | tf_op jit(solution)/shard_map/ppermute | solution.py:144
  606.9 42.7 %collective-permute-start.45 = (bf16[256,768]{1,0:T(8,128)(2,1)S(1)}, bf16[256,768]{1,0:T(8,128)(2,1)S(1)}, u32[]{:S(2)}, u32[]{:S(2)}) collective-permute-start(bf16[256,768]{1,0:T(8,128)(2,1)S(1)} %add_convert_fusion.22), channel_id=1, source_target_pairs={{12,8},{8,4},{4,0},{13,9},{9,5},{5,1},{14,10},{10,6},{6,2},{15,11}... | collective-permute-start | bytes 1179656 | tf_op jit(solution)/shard_map/ppermute | solution.py:144
  609.6 92.3 %collective-permute-start.71 = (bf16[256,2048]{1,0:T(8,128)(2,1)S(1)}, bf16[256,2048]{1,0:T(8,128)(2,1)S(1)}, u32[]{:S(2)}, u32[]{:S(2)}) collective-permute-start(bf16[256,2048]{1,0:T(8,128)(2,1)S(1)} %get-tuple-element.38), channel_id=1, source_target_pairs={{0,4},{4,8},{8,12},{1,5},{5,9},{9,13},{2,6},{6,10},{10,14},{3,7},{... | collective-permute-start | bytes 3145736 | tf_op jit(solution)/shard_map/ppermute | solution.py:141
  652.1 47.9 %collective-permute-start.67 = (bf16[256,2048]{1,0:T(8,128)(2,1)S(1)}, bf16[256,2048]{1,0:T(8,128)(2,1)S(1)}, u32[]{:S(2)}, u32[]{:S(2)}) collective-permute-start(bf16[256,2048]{1,0:T(8,128)(2,1)S(1)} %add_convert_fusion.12), channel_id=1, source_target_pairs={{12,8},{8,4},{4,0},{13,9},{9,5},{5,1},{14,10},{10,6},{6,2},{15,11}... | collective-permute-start | bytes 3145736 | tf_op jit(solution)/shard_map/ppermute | solution.py:144
  655.6 68.7 %collective-permute-start.82 = (bf16[2048,256]{1,0:T(8,128)(2,1)S(1)}, bf16[2048,256]{1,0:T(8,128)(2,1)S(1)}, u32[]{:S(2)}, u32[]{:S(2)}) collective-permute-start(bf16[2048,256]{1,0:T(8,128)(2,1)S(1)} %get-tuple-element.34), channel_id=1, source_target_pairs={{0,4},{4,8},{8,12},{1,5},{5,9},{9,13},{2,6},{6,10},{10,14},{3,7},{... | collective-permute-start | bytes 3145736 | tf_op jit(solution)/shard_map/ppermute | solution.py:141
  677.6 44.9 %collective-permute-start.74 = (bf16[256,2048]{1,0:T(8,128)(2,1)S(1)}, bf16[256,2048]{1,0:T(8,128)(2,1)S(1)}, u32[]{:S(2)}, u32[]{:S(2)}) collective-permute-start(bf16[256,2048]{1,0:T(8,128)(2,1)S(1)} %add_convert_fusion.8), channel_id=1, source_target_pairs={{12,8},{8,4},{4,0},{13,9},{9,5},{5,1},{14,10},{10,6},{6,2},{15,11}... | collective-permute-start | bytes 3145736 | tf_op jit(solution)/shard_map/ppermute | solution.py:144
  679.9 58.6 %collective-permute-start.85 = (bf16[2048,256]{1,0:T(8,128)(2,1)S(1)}, bf16[2048,256]{1,0:T(8,128)(2,1)S(1)}, u32[]{:S(2)}, u32[]{:S(2)}) collective-permute-start(bf16[2048,256]{1,0:T(8,128)(2,1)S(1)} %add_convert_fusion.4), channel_id=1, source_target_pairs={{12,8},{8,4},{4,0},{13,9},{9,5},{5,1},{14,10},{10,6},{6,2},{15,11}... | collective-permute-start | bytes 3145736 | tf_op jit(solution)/shard_map/ppermute | solution.py:144
  (159 other events, 2438.4 us)
